TPU v7x, 256 devices: a whole 4x4x8 slice. The times are simulated.
256 devices in a mesh: layer: 4 (over z_hi, core), query: 4 (over z_lo), doc: 16 (over y, x).
Axes of the slice: x: 4, y: 4, z: 8 (z_hi: 2, z_lo: 4; z = z_hi * 4 + z_lo), core: 2. Of those that a mesh axis runs over, the one named last changes fastest.
Arguments:
- query_out: bfloat16 [256, 11008], P(None, 'doc'), may hold values from -0.21875 to 0.21875
- query_in: bfloat16 [256, 4096], P(None, 'doc'), may hold values from -0.21875 to 0.21875
- basis_out: bfloat16 [11008, 11008], P('doc', 'layer'), may hold values from -0.0546875 to 0.0546875
- basis_in: bfloat16 [4096, 4096], P('doc', 'query'), may hold values from -0.09375 to 0.09375
- eigenvalues: bfloat16 [11008, 4096], P('layer', ('query', 'doc')), may hold values from 0.049804688 to 5
- doc_out: bfloat16 [64, 64, 11008], P('doc', None, 'layer'), may hold values from -0.21875 to 0.21875
- doc_in: bfloat16 [64, 64, 4096], P('doc', None, 'query'), may hold values from -0.21875 to 0.21875
- pair_list: int32 [64, 2], P('doc'), may hold values from 0 to 3, as said below
- pair_count: int32 [16], P('doc'), may hold values from 1 to 4, as said below
Outputs:
- scores: float32 [64, 4], P('doc')
Inputs may be any that keep to these rules, and one draw needn't show every extreme that they name: `pair_list`: A row of a doc device's list is live when its position is below that device's count; column 0 is a query block below 4, column 1 one of the device's own 4 blocks; rows past the count hold ids in the same ranges and are ignored. `pair_count`: one doc device holds exactly 4 live slots in every draw.
All inputs are finite; a program needn't handle non-finite values.
Results may differ from a plain program's by a relative error of at most 0.0063.
Values may be sent and summed in bfloat16 or wider, within the bound.
No kernel may reach another device: no remote copies, remote signals or barrier semaphores. Data moves between devices by JAX's collectives and lax.ppermute only.
A program may use at most 128 MiB of HBM per device.

v0:
```python
import jax
import jax.numpy as jnp
from jax import lax
from jax.sharding import PartitionSpec as P

FACTOR_RANK = 32
QUERY_BLOCK = 2
DOC_BLOCK = 2


damping = 0.1


def local(
    query_out, query_in, basis_out, basis_in, eigenvalues, doc_out, doc_in, pair_list, pair_count
):
    rows_tile = basis_out.shape[1]
    part_out = jnp.dot(query_out, basis_out, preferred_element_type=jnp.float32)
    part_in = jnp.dot(query_in, basis_in, preferred_element_type=jnp.float32)
    summed_out, summed_in = lax.psum((part_out, part_in), "doc")
    rotated_out = summed_out.astype(jnp.bfloat16)
    rotated_in = summed_in.astype(jnp.bfloat16)
    slot_total = pair_list.shape[0]
    local_docs = jnp.concatenate([doc_out, doc_in], axis=2)
    query_ids = pair_list[:, 0]
    slot_data = jnp.take(local_docs, pair_list[:, 1], axis=0)
    live_count = pair_count[0]
    block_rows = QUERY_BLOCK * FACTOR_RANK
    band_rows = rows_tile // 4
    empty = jnp.zeros((slot_total, QUERY_BLOCK, DOC_BLOCK), jnp.float32)
    piece_cols = lax.all_gather(eigenvalues, "doc", axis=1, tiled=True)
    piece_width = piece_cols.shape[1]
    weights = 1.0 / (piece_cols.astype(jnp.float32) + damping)

    def one_slot(slot_index, running):
        chosen_query = query_ids[slot_index]
        q_out = lax.dynamic_slice_in_dim(rotated_out, chosen_query * block_rows, block_rows, 0)
        q_out = q_out.reshape(QUERY_BLOCK, FACTOR_RANK, rows_tile)
        q_in = lax.dynamic_slice_in_dim(rotated_in, chosen_query * block_rows, block_rows, 0)
        q_in = q_in.reshape(QUERY_BLOCK, FACTOR_RANK, piece_width)
        single = lax.dynamic_index_in_dim(slot_data, slot_index, 0, keepdims=False)
        d_out = single[:, :rows_tile].reshape(DOC_BLOCK, FACTOR_RANK, rows_tile)
        d_in = single[:, rows_tile:]
        d_in = d_in.reshape(DOC_BLOCK, FACTOR_RANK, piece_width)
        result = jnp.zeros((QUERY_BLOCK, DOC_BLOCK), jnp.float32)
        for band_index in range(4):
            row_start = band_index * band_rows
            row_end = row_start + band_rows
            precond = jnp.einsum(
                "qri,qrj->qij",
                q_out[:, :, row_start:row_end],
                q_in,
                preferred_element_type=jnp.float32,
            )
            precond = (precond * weights[row_start:row_end]).astype(jnp.bfloat16)
            doc_matrix = jnp.einsum(
                "dri,drj->dij",
                d_out[:, :, row_start:row_end],
                d_in,
                preferred_element_type=jnp.float32,
            ).astype(jnp.bfloat16)
            result = result + jnp.einsum(
                "qij,dij->qd", precond, doc_matrix, preferred_element_type=jnp.float32
            )
        current = lax.dynamic_index_in_dim(running, slot_index, 0, keepdims=False)
        return lax.dynamic_update_index_in_dim(running, current + result, slot_index, 0)

    partial_scores = lax.fori_loop(0, live_count, one_slot, empty)
    flat_scores = partial_scores.reshape(slot_total, QUERY_BLOCK * DOC_BLOCK)
    is_live = jnp.arange(slot_total, dtype=jnp.int32) < live_count
    flat_scores = jnp.where(is_live[:, None], flat_scores, 0.0)
    return lax.psum(flat_scores, ("layer", "query"))


def solution(mesh):
    in_specs = (
        P(None, "doc"),
        P(None, "doc"),
        P("doc", "layer"),
        P("doc", "query"),
        P("layer", ("query", "doc")),
        P("doc", None, "layer"),
        P("doc", None, "query"),
        P("doc", None),
        P("doc"),
    )
    out_specs = P("doc", None)
    return jax.shard_map(local, mesh=mesh, in_specs=in_specs, out_specs=out_specs, check_vma=False)
```

profile of v0, /device:TPU:5, one launch (start us, length us, event | category | flops | bytes accessed | tf_op | source)
XLA Modules:
  0.0 572.8 jit_solution(9879662846530065742)
XLA Ops:
  7.3 4.0 fusion.61
  11.3 1.3 fusion.62
  12.6 118.9 %all-reduce.2 = (bf16[256,2752]{0,1:T(8,128)(2,1)}, bf16[256,1024]{1,0:T(8,128)(2,1)}) all-reduce(f32[256,2752]{0,1:T(8,128)S(1)} %fusion.61, f32[256,1024]{1,0:T(8,128)} %fusion.62), channel_id=1, replica_groups=mesh['layer'=4,'query'=4,'doc'=16] {'doc'}, use_global_device_ids=true, to_apply=%region_0.0 | all-reduce | flops 966656 | bytes 5799936 | tf_op jit(solution)/shard_map/psum | solution.py:20
  131.5 2.7 copy.14
  134.9 1.6 pad_maximum_fusion
  136.5 2.2 gather_fusion
  139.2 1.5 broadcast_select_fusion
  140.7 8.4 %add_divide_fusion = f32[2752,1024]{0,1:T(8,128)} fusion(bf16[2752,1024]{0,1:T(8,128)(2,1)} %all-gather.2.cloned.1.call-done), kind=kLoop, calls=%fused_computation.48 | loop fusion | flops 8454144 | bytes 16908288 | tf_op jit(solution)/shard_map/div | solution.py:33
  149.1 11.9 %copy.15 = f32[2752,1024]{1,0:T(8,128)} copy(f32[2752,1024]{0,1:T(8,128)} %add_divide_fusion) | data formatting | bytes 22544384 | tf_op jit(solution)/shard_map/while | solution.py:68
  161.0 369.3 %while.10 = (s32[]{:T(128)}, f32[4,2,2]{2,1,0:T(2,128)S(1)}, s32[]{:T(128)}, s32[4]{0:T(128)S(1)}, bf16[256,2752]{1,0:T(8,128)(2,1)}, /*index=5*/bf16[256,1024]{...) while((s32[]{:T(128)}, f32[4,2,2]{2,1,0:T(2,128)S(1)}, ...), condition=%wide.region_3.4_spmd, body=%wide.region_2.3_spmd.sunk | while | flops 755236864 | bytes 109008240 | solution.py:68
  165.3 3.6 fusion.135
  170.7 1.1 fusion.134
  171.8 9.7 %fusion.132 = (f32[688,1024]{1,0:T(8,128)}, f32[688,1024]{1,0:T(8,128)}, f32[688,1024]{1,0:T(8,128)}, f32[688,1024]{1,0:T(8,128)}) fusion(f32[2752,1024]{1,0:T(8,128)} %get-tuple-element.179), kind=kLoop, calls=%fused_computation.58.clone.1 | loop fusion | bytes 22544384 | tf_op jit(solution)/shard_map/while/body/slice | solution.py:55
  181.5 12.9 %fusion.136 = f32[2,2]{1,0:T(2,128)S(1)} fusion(bf16[2,688,1024]{2,1,0:T(8,128)(2,1)S(1)} %fusion.134, f32[2,688,1024]{2,1,0:T(8,128)} %fusion.135, f32[688,1024]{1,0:T(8,128)} %get-tuple-element.144), kind=kOutput, calls=%fused_computation.18.clone.1 | convolution fusion | flops 8454144 | bytes 11272208 | tf_op jit(solution)/shard_map/while/body/qij,dij->qd/dot_general | solution.py:62
  194.3 4.5 fusion.138
  198.8 2.0 fusion.137
  200.8 13.5 %fusion.139 = f32[2,2]{1,0:T(2,128)S(1)} fusion(bf16[2,688,1024]{2,1,0:T(8,128)(2,1)S(1)} %fusion.137, f32[2,688,1024]{2,1,0:T(8,128)} %fusion.138, f32[688,1024]{1,0:T(8,128)} %get-tuple-element.145), kind=kOutput, calls=%fused_computation.19.clone.1 | convolution fusion | flops 8454144 | bytes 11272208 | tf_op jit(solution)/shard_map/while/body/qij,dij->qd/dot_general | solution.py:62
  214.3 4.5 fusion.131
  218.7 2.0 fusion.130
  220.7 13.0 %fusion.133 = f32[2,2]{1,0:T(2,128)S(1)} fusion(bf16[2,688,1024]{2,1,0:T(8,128)(2,1)S(1)} %fusion.130, f32[2,688,1024]{2,1,0:T(8,128)} %fusion.131, f32[688,1024]{1,0:T(8,128)} %get-tuple-element.143), kind=kOutput, calls=%fused_computation.17.clone.1 | convolution fusion | flops 8454144 | bytes 11272208 | tf_op jit(solution)/shard_map/while/body/qij,dij->qd/dot_general | solution.py:62
  233.8 4.3 fusion.141
  238.1 1.8 fusion.140
  239.9 12.9 %fusion.142 = f32[4,2,2]{2,1,0:T(2,128)S(1)} fusion(f32[4,2,2]{2,1,0:T(2,128)S(1)} %get-tuple-element.161, s32[]{:T(128)S(6)} %select_n.40, f32[2,2]{1,0:T(2,128)S(1)} %fusion.129, f32[2,2]{1,0:T(2,128)S(1)} %fusion.133, f32[2,2]{1,0:T(2,128)S(1)} %fusion.136, f32[2,2]{1,0:T(2,128)S(1)} %fusion.139, bf16[2,688,1024]{2,1,0:T(8,128)(2,1)S(1)} %fusion.140, ...), kind=kOutput, calls=%fused_computation.26.clone.1 | convolution fusion | flops 8454160 | bytes 11277316 | tf_op jit(solution)/shard_map/while/body/qij,dij->qd/dot_general | solution.py:62
  257.2 3.6 fusion.135
  260.8 1.1 dynamic-slice_bitcast_fusion.2
  262.6 1.1 fusion.134
  263.7 9.7 %fusion.132 = (f32[688,1024]{1,0:T(8,128)}, f32[688,1024]{1,0:T(8,128)}, f32[688,1024]{1,0:T(8,128)}, f32[688,1024]{1,0:T(8,128)}) fusion(f32[2752,1024]{1,0:T(8,128)} %get-tuple-element.179), kind=kLoop, calls=%fused_computation.58.clone.1 | loop fusion | bytes 22544384 | tf_op jit(solution)/shard_map/while/body/slice | solution.py:55
  273.4 12.9 %fusion.136 = f32[2,2]{1,0:T(2,128)S(1)} fusion(bf16[2,688,1024]{2,1,0:T(8,128)(2,1)S(1)} %fusion.134, f32[2,688,1024]{2,1,0:T(8,128)} %fusion.135, f32[688,1024]{1,0:T(8,128)} %get-tuple-element.144), kind=kOutput, calls=%fused_computation.18.clone.1 | convolution fusion | flops 8454144 | bytes 11272208 | tf_op jit(solution)/shard_map/while/body/qij,dij->qd/dot_general | solution.py:62
  286.2 4.5 fusion.138
  290.7 2.0 fusion.137
  292.7 13.0 %fusion.139 = f32[2,2]{1,0:T(2,128)S(1)} fusion(bf16[2,688,1024]{2,1,0:T(8,128)(2,1)S(1)} %fusion.137, f32[2,688,1024]{2,1,0:T(8,128)} %fusion.138, f32[688,1024]{1,0:T(8,128)} %get-tuple-element.145), kind=kOutput, calls=%fused_computation.19.clone.1 | convolution fusion | flops 8454144 | bytes 11272208 | tf_op jit(solution)/shard_map/while/body/qij,dij->qd/dot_general | solution.py:62
  305.7 4.5 fusion.131
  310.2 2.0 fusion.130
  312.2 13.3 %fusion.133 = f32[2,2]{1,0:T(2,128)S(1)} fusion(bf16[2,688,1024]{2,1,0:T(8,128)(2,1)S(1)} %fusion.130, f32[2,688,1024]{2,1,0:T(8,128)} %fusion.131, f32[688,1024]{1,0:T(8,128)} %get-tuple-element.143), kind=kOutput, calls=%fused_computation.17.clone.1 | convolution fusion | flops 8454144 | bytes 11272208 | tf_op jit(solution)/shard_map/while/body/qij,dij->qd/dot_general | solution.py:62
  325.5 4.3 fusion.141
  329.7 1.8 fusion.140
  331.6 12.9 %fusion.142 = f32[4,2,2]{2,1,0:T(2,128)S(1)} fusion(f32[4,2,2]{2,1,0:T(2,128)S(1)} %get-tuple-element.161, s32[]{:T(128)S(6)} %select_n.40, f32[2,2]{1,0:T(2,128)S(1)} %fusion.129, f32[2,2]{1,0:T(2,128)S(1)} %fusion.133, f32[2,2]{1,0:T(2,128)S(1)} %fusion.136, f32[2,2]{1,0:T(2,128)S(1)} %fusion.139, bf16[2,688,1024]{2,1,0:T(8,128)(2,1)S(1)} %fusion.140, ...), kind=kOutput, calls=%fused_computation.26.clone.1 | convolution fusion | flops 8454160 | bytes 11277316 | tf_op jit(solution)/shard_map/while/body/qij,dij->qd/dot_general | solution.py:62
  348.7 3.6 fusion.135
  354.1 1.1 fusion.134
  355.2 9.7 %fusion.132 = (f32[688,1024]{1,0:T(8,128)}, f32[688,1024]{1,0:T(8,128)}, f32[688,1024]{1,0:T(8,128)}, f32[688,1024]{1,0:T(8,128)}) fusion(f32[2752,1024]{1,0:T(8,128)} %get-tuple-element.179), kind=kLoop, calls=%fused_computation.58.clone.1 | loop fusion | bytes 22544384 | tf_op jit(solution)/shard_map/while/body/slice | solution.py:55
  364.8 12.9 %fusion.136 = f32[2,2]{1,0:T(2,128)S(1)} fusion(bf16[2,688,1024]{2,1,0:T(8,128)(2,1)S(1)} %fusion.134, f32[2,688,1024]{2,1,0:T(8,128)} %fusion.135, f32[688,1024]{1,0:T(8,128)} %get-tuple-element.144), kind=kOutput, calls=%fused_computation.18.clone.1 | convolution fusion | flops 8454144 | bytes 11272208 | tf_op jit(solution)/shard_map/while/body/qij,dij->qd/dot_general | solution.py:62
  377.7 4.5 fusion.138
  382.2 2.0 fusion.137
  384.2 13.3 %fusion.139 = f32[2,2]{1,0:T(2,128)S(1)} fusion(bf16[2,688,1024]{2,1,0:T(8,128)(2,1)S(1)} %fusion.137, f32[2,688,1024]{2,1,0:T(8,128)} %fusion.138, f32[688,1024]{1,0:T(8,128)} %get-tuple-element.145), kind=kOutput, calls=%fused_computation.19.clone.1 | convolution fusion | flops 8454144 | bytes 11272208 | tf_op jit(solution)/shard_map/while/body/qij,dij->qd/dot_general | solution.py:62
  397.4 4.5 fusion.131
  401.9 2.0 fusion.130
  403.9 13.0 %fusion.133 = f32[2,2]{1,0:T(2,128)S(1)} fusion(bf16[2,688,1024]{2,1,0:T(8,128)(2,1)S(1)} %fusion.130, f32[2,688,1024]{2,1,0:T(8,128)} %fusion.131, f32[688,1024]{1,0:T(8,128)} %get-tuple-element.143), kind=kOutput, calls=%fused_computation.17.clone.1 | convolution fusion | flops 8454144 | bytes 11272208 | tf_op jit(solution)/shard_map/while/body/qij,dij->qd/dot_general | solution.py:62
  416.9 4.3 fusion.141
  421.2 1.8 fusion.140
  423.0 12.9 %fusion.142 = f32[4,2,2]{2,1,0:T(2,128)S(1)} fusion(f32[4,2,2]{2,1,0:T(2,128)S(1)} %get-tuple-element.161, s32[]{:T(128)S(6)} %select_n.40, f32[2,2]{1,0:T(2,128)S(1)} %fusion.129, f32[2,2]{1,0:T(2,128)S(1)} %fusion.133, f32[2,2]{1,0:T(2,128)S(1)} %fusion.136, f32[2,2]{1,0:T(2,128)S(1)} %fusion.139, bf16[2,688,1024]{2,1,0:T(8,128)(2,1)S(1)} %fusion.140, ...), kind=kOutput, calls=%fused_computation.26.clone.1 | convolution fusion | flops 8454160 | bytes 11277316 | tf_op jit(solution)/shard_map/while/body/qij,dij->qd/dot_general | solution.py:62
  440.4 3.6 fusion.135
  445.8 1.1 fusion.134
  446.9 9.7 %fusion.132 = (f32[688,1024]{1,0:T(8,128)}, f32[688,1024]{1,0:T(8,128)}, f32[688,1024]{1,0:T(8,128)}, f32[688,1024]{1,0:T(8,128)}) fusion(f32[2752,1024]{1,0:T(8,128)} %get-tuple-element.179), kind=kLoop, calls=%fused_computation.58.clone.1 | loop fusion | bytes 22544384 | tf_op jit(solution)/shard_map/while/body/slice | solution.py:55
  456.5 12.9 %fusion.136 = f32[2,2]{1,0:T(2,128)S(1)} fusion(bf16[2,688,1024]{2,1,0:T(8,128)(2,1)S(1)} %fusion.134, f32[2,688,1024]{2,1,0:T(8,128)} %fusion.135, f32[688,1024]{1,0:T(8,128)} %get-tuple-element.144), kind=kOutput, calls=%fused_computation.18.clone.1 | convolution fusion | flops 8454144 | bytes 11272208 | tf_op jit(solution)/shard_map/while/body/qij,dij->qd/dot_general | solution.py:62
  469.4 4.5 fusion.138
  473.9 2.0 fusion.137
  475.9 13.0 %fusion.139 = f32[2,2]{1,0:T(2,128)S(1)} fusion(bf16[2,688,1024]{2,1,0:T(8,128)(2,1)S(1)} %fusion.137, f32[2,688,1024]{2,1,0:T(8,128)} %fusion.138, f32[688,1024]{1,0:T(8,128)} %get-tuple-element.145), kind=kOutput, calls=%fused_computation.19.clone.1 | convolution fusion | flops 8454144 | bytes 11272208 | tf_op jit(solution)/shard_map/while/body/qij,dij->qd/dot_general | solution.py:62
  488.9 4.5 fusion.131
  493.4 2.0 fusion.130
  495.4 13.3 %fusion.133 = f32[2,2]{1,0:T(2,128)S(1)} fusion(bf16[2,688,1024]{2,1,0:T(8,128)(2,1)S(1)} %fusion.130, f32[2,688,1024]{2,1,0:T(8,128)} %fusion.131, f32[688,1024]{1,0:T(8,128)} %get-tuple-element.143), kind=kOutput, calls=%fused_computation.17.clone.1 | convolution fusion | flops 8454144 | bytes 11272208 | tf_op jit(solution)/shard_map/while/body/qij,dij->qd/dot_general | solution.py:62
  508.6 4.3 fusion.141
  512.9 1.8 fusion.140
  514.7 12.9 %fusion.142 = f32[4,2,2]{2,1,0:T(2,128)S(1)} fusion(f32[4,2,2]{2,1,0:T(2,128)S(1)} %get-tuple-element.161, s32[]{:T(128)S(6)} %select_n.40, f32[2,2]{1,0:T(2,128)S(1)} %fusion.129, f32[2,2]{1,0:T(2,128)S(1)} %fusion.133, f32[2,2]{1,0:T(2,128)S(1)} %fusion.136, f32[2,2]{1,0:T(2,128)S(1)} %fusion.139, bf16[2,688,1024]{2,1,0:T(8,128)(2,1)S(1)} %fusion.140, ...), kind=kOutput, calls=%fused_computation.26.clone.1 | convolution fusion | flops 8454160 | bytes 11277316 | tf_op jit(solution)/shard_map/while/body/qij,dij->qd/dot_general | solution.py:62
  530.4 34.6 %psum.23 = f32[4,4]{0,1:T(4,128)S(1)} all-reduce(f32[4,4]{0,1:T(4,128)S(1)} %broadcast_select_fusion.1), channel_id=1, replica_groups=mesh['layer'=4,'query'=4,'doc'=16] {'layer','query'}, use_global_device_ids=true, to_apply=%region_4.5 | all-reduce | flops 16 | bytes 128 | tf_op jit(solution)/shard_map/psum | solution.py:72
  (68 shorter events, 19.0 us)
Async XLA Ops:
  6.5 4.7 copy-start
  6.5 134.2 %all-gather.2.cloned.1.call-start = ((), (), s32[]{:S(2)}) async-start(), calls=%async_computation | async-start | bytes 6127616 | tf_op jit(solution)/shard_map/all_gather | solution.py:31
  7.3 4.0 copy-start.6
  12.6 122.2 %copy-start.7 = (s32[4,2]{0,1:T(2,128)S(1)}, s32[4,2]{0,1:T(2,128)}, u32[]{:S(2)}) copy-start(s32[4,2]{0,1:T(2,128)} %param.18) | copy-start | bytes 100
  12.6 122.3 %copy-start.5 = (bf16[4,64,1024]{2,1,0:T(8,128)(2,1)S(1)}, bf16[4,64,1024]{2,1,0:T(8,128)(2,1)}, u32[]{:S(2)}) copy-start(bf16[4,64,1024]{2,1,0:T(8,128)(2,1)} %param.17) | copy-start | bytes 1572868
  131.5 3.4 copy-start.4
  161.0 369.4 %copy-start.8 = (pred[4]{0:T(512)(128)(4,1)S(1)}, pred[4]{0:T(512)(128)(4,1)}, u32[]{:S(2)}) copy-start(pred[4]{0:T(512)(128)(4,1)} %iota_compare_fusion) | copy-start | bytes 16
  164.2 4.6 copy-start.3
  169.9 0.7 copy-start.2
  256.2 4.6 copy-start.3
  261.9 0.7 copy-start.2
  347.6 4.6 copy-start.3
  353.3 0.7 copy-start.2
  439.3 4.6 copy-start.3
  445.0 0.7 copy-start.2
  530.3 35.4 %copy-start.1 = (bf16[256,1024]{1,0:T(8,128)(2,1)S(1)}, bf16[256,1024]{1,0:T(8,128)(2,1)}, u32[]{:S(2)}) copy-start(bf16[256,1024]{1,0:T(8,128)(2,1)} %param.14) | copy-start | bytes 1572868
Sparse Core Ops, SparseCore 0:
  9.8 118.4 all-gather.1
where the time goes:
time: 579 us; the launch traced here: 573 us
  matrix products  309 us (53%)
  blocking collectives  154 us (27%)
  local copies, waits for them, and re-layouts  74.2 us (13%)
  between operations  14.4 us (2%)
  other arithmetic  12 us (2%)
  loops' own time  9.37 us (2%)
    dot_general x16, matrix products, one_slot(): jnp.einsum('qij,dij->qd', precond, doc_matrix, preferred_element_type=jnp...  209 us
    psum x1, blocking collectives, local(): summed_out, summed_in = lax.psum((part_out, part_in), 'doc')  119 us
    dot_general x16, matrix products, one_slot(): jnp.einsum('qri,qrj->qij', q_out[:, :, row_start:row_end], q_in, preferre...  67 us
    slice x4, local copies, waits for them, and re-layouts, one_slot(): precond = (precond * weights[row_start:row_end]).astype(jnp.bfloat16)  38.6 us
    psum x1, blocking collectives, local(): return lax.psum(flat_scores, ('layer', 'query'))  34.6 us
    dot_general x16, matrix products, one_slot(): jnp.einsum('dri,drj->dij', d_out[:, :, row_start:row_end], d_in, preferre...  27.7 us
    while x3, local copies, waits for them, and re-layouts, local(): partial_scores = lax.fori_loop(0, live_count, one_slot, empty)  14.6 us
  transfers between devices with their start and end apart: 1, of which 0 were waited for; matrix products, arithmetic and copies ran while one was open for 2% of the time, Pallas kernels for 0%

commit v1 on v0

v1 whole, which is shorter than its diff:
```python
import functools

import jax
import jax.numpy as jnp
from jax import lax
from jax.experimental import pallas as pl
from jax.experimental.pallas import tpu as pltpu
from jax.sharding import PartitionSpec as P

FACTOR_RANK = 32
QUERY_BLOCK = 2
DOC_BLOCK = 2
BAND = 256
TILE = 256
LANES = 128
SCALE = 4096.0

damping = 0.1


def score_kernel(
    pairs_ref, count_ref, rows_ref, band_ref, eig_ref, out_ref, in_ref, scores_ref,
    weights, doc_rows, scaled, total,
):
    step = pl.program_id(0)
    queries = rows_ref.shape[0]
    band = eig_ref.shape[0]
    width = eig_ref.shape[1]
    padded = doc_rows.shape[1]
    first = rows_ref.shape[1] - width
    block_rows = QUERY_BLOCK * FACTOR_RANK
    docs = out_ref.shape[0] * out_ref.shape[1]
    slots = pairs_ref.shape[0]
    live = count_ref[0]

    @pl.when(step == 0)
    def _():
        total[...] = jnp.zeros_like(total)
        start = width // LANES * LANES
        doc_rows[:, start:] = jnp.zeros((docs, padded - start), jnp.bfloat16)
        scaled[:, start:] = jnp.zeros((scaled.shape[0], padded - start), jnp.bfloat16)
        for block in range(out_ref.shape[0]):
            rows = slice(block * block_rows, (block + 1) * block_rows)
            doc_rows[rows, :width] = out_ref[block]

    shifted = eig_ref[...].astype(jnp.float32) + damping
    guess = pl.reciprocal(shifted, approx=True)
    weights[...] = guess * (2.0 - shifted * guess)

    band_rows = band_ref[...].astype(jnp.float32).T
    doc_side = jnp.concatenate([in_ref[block] for block in range(in_ref.shape[0])], axis=0)
    doc_side = doc_side.astype(jnp.float32).T
    lane = lax.broadcasted_iota(jnp.int32, (band, queries), 1) // FACTOR_RANK

    for block in range(queries // block_rows):
        wanted = jnp.bool_(False)
        for slot in range(slots):
            wanted = wanted | ((pairs_ref[slot, 0] == block) & (live > slot))

        @pl.when(wanted)
        def _():
            left = jnp.concatenate(
                [
                    jnp.where(lane == block * QUERY_BLOCK + q, band_rows, 0.0)
                    for q in range(QUERY_BLOCK)
                ],
                axis=0,
            ).astype(jnp.bfloat16)
            for begin in range(0, width, TILE):
                end = min(begin + TILE, width)
                product = jnp.dot(
                    left, rows_ref[:, first + begin:first + end], preferred_element_type=jnp.float32
                )
                for q in range(QUERY_BLOCK):
                    part = slice(q * band, (q + 1) * band)
                    scaled[part, begin:end] = (product[part] * weights[:, begin:end]).astype(jnp.bfloat16)
            mixed = lax.dot_general(
                scaled[...], doc_rows[...], (((1,), (1,)), ((), ())),
                preferred_element_type=jnp.float32,
            )
            for q in range(QUERY_BLOCK):
                part = mixed[q * band:(q + 1) * band] * doc_side
                row = block * QUERY_BLOCK + q
                total[row:row + 1, :] += jnp.sum(part, axis=0, keepdims=True)

    @pl.when(step == pl.num_programs(0) - 1)
    def _():
        shape = total.shape
        row = lax.broadcasted_iota(jnp.int32, shape, 0)
        column = lax.broadcasted_iota(jnp.int32, shape, 1)
        flat = scores_ref.shape
        out_row = lax.broadcasted_iota(jnp.int32, flat, 0)
        out_column = lax.broadcasted_iota(jnp.int32, flat, 1)
        result = jnp.zeros(flat, jnp.float32)
        for slot in range(slots):
            for q in range(QUERY_BLOCK):
                chosen = row == pairs_ref[slot, 0] * QUERY_BLOCK + q
                for d in range(DOC_BLOCK):
                    doc = pairs_ref[slot, 1] * DOC_BLOCK + d
                    inside = chosen & (column // FACTOR_RANK == doc) & (live > slot)
                    value = jnp.sum(jnp.where(inside, total[...], 0.0))
                    here = (out_row == slot * QUERY_BLOCK + q) & (out_column == d)
                    result = jnp.where(here, value, result)
        scores_ref[...] = result


def slot_scores(pairs, count, rows, eigen_rows, doc_out, doc_in):
    queries = rows.shape[0]
    model, width = eigen_rows.shape
    blocks, block_rows, _ = doc_out.shape
    padded = -(-width // TILE) * TILE
    out_rows = pairs.shape[0] * QUERY_BLOCK
    return pl.pallas_call(
        score_kernel,
        out_shape=jax.ShapeDtypeStruct((out_rows, LANES), jnp.float32),
        grid_spec=pltpu.PrefetchScalarGridSpec(
            num_scalar_prefetch=2,
            grid=(model // BAND,),
            in_specs=[
                pl.BlockSpec(rows.shape, lambda j, *_: (0, 0)),
                pl.BlockSpec((queries, BAND), lambda j, *_: (0, j)),
                pl.BlockSpec((BAND, width), lambda j, *_: (j, 0)),
                pl.BlockSpec(doc_out.shape, lambda j, *_: (0, 0, 0)),
                pl.BlockSpec((blocks, block_rows, BAND), lambda j, *_: (0, 0, j)),
            ],
            out_specs=pl.BlockSpec((out_rows, LANES), lambda j, *_: (0, 0)),
            scratch_shapes=[
                pltpu.VMEM((BAND, width), jnp.float32),
                pltpu.VMEM((blocks * block_rows, padded), jnp.bfloat16),
                pltpu.VMEM((QUERY_BLOCK * BAND, padded), jnp.bfloat16),
                pltpu.VMEM((queries // FACTOR_RANK, blocks * block_rows), jnp.float32),
            ],
        ),
        compiler_params=pltpu.CompilerParams(
            dimension_semantics=("arbitrary",), vmem_limit_bytes=48 * 2**20
        ),
        cost_estimate=pl.CostEstimate(
            flops=4 * model * width * 256 * 8, bytes_accessed=10 * 2**20, transcendentals=0
        ),
    )(pairs, count, rows, rows, eigen_rows, doc_out, doc_in)


def local(
    query_out, query_in, basis_out, basis_in, eigenvalues, doc_out, doc_in, pair_list, pair_count
):
    eigen_rows = lax.all_gather(eigenvalues.T, "doc", axis=0, tiled=True)
    parts = lax.axis_size("doc")
    queries = query_out.shape[0]
    share = queries // parts
    part_in = jnp.dot(query_in, basis_in, preferred_element_type=jnp.float32)
    part_out = jnp.dot(query_out, basis_out, preferred_element_type=jnp.float32)
    partial = jnp.concatenate([part_in, part_out], axis=1)
    width = partial.shape[1]
    sent = (partial * SCALE).astype(jnp.float16).reshape(parts, share, width)
    received = lax.all_to_all(sent, "doc", 0, 0)
    own = (jnp.sum(received.astype(jnp.float32), axis=0) * (1.0 / SCALE)).astype(jnp.bfloat16)
    copies = jnp.broadcast_to(own[None], (parts, share, width))
    rows = lax.all_to_all(copies, "doc", 0, 0).reshape(queries, width)
    scores = slot_scores(pair_list, pair_count, rows, eigen_rows, doc_out, doc_in)
    group = lax.axis_size("layer") * lax.axis_size("query")
    copies = jnp.broadcast_to(scores[None], (group,) + scores.shape)
    summed = jnp.sum(lax.all_to_all(copies, ("layer", "query"), 0, 0), axis=0)
    return summed[:, :DOC_BLOCK].reshape(pair_list.shape[0], QUERY_BLOCK * DOC_BLOCK)


def solution(mesh):
    in_specs = (
        P(None, "doc"),
        P(None, "doc"),
        P("doc", "layer"),
        P("doc", "query"),
        P("layer", ("query", "doc")),
        P("doc", None, "layer"),
        P("doc", None, "query"),
        P("doc", None),
        P("doc"),
    )
    out_specs = P("doc", None)
    return jax.shard_map(local, mesh=mesh, in_specs=in_specs, out_specs=out_specs, check_vma=False)
```

time: 579 us -> 159 us (0.27)
  the two profiles are of different devices: /device:TPU:5 before, /device:TPU:3 now
where the time goes in v1:
time: 159 us
  blocking collectives  53.8 us (34%)
  waiting for transfers between devices  48.6 us (31%)
  Pallas kernels  28.2 us (18%)
  between operations  14.1 us (9%)
  starting transfers between devices  4.78 us (3%)
  matrix products  4.74 us (3%)
  local copies, waits for them, and re-layouts  3.85 us (2%)
    all_to_all x1, blocking collectives, local(): received = lax.all_to_all(sent, 'doc', 0, 0)  37.4 us
    all_to_all x1, waiting for transfers between devices, local(): rows = lax.all_to_all(copies, 'doc', 0, 0).reshape(queries, width)  36.8 us
    pallas_call x1, Pallas kernels, slot_scores(): pl.pallas_call(score_kernel, out_shape=jax.ShapeDtypeStruct((out_rows, LA...  28.2 us
    all_to_all x1, blocking collectives, local(): summed = jnp.sum(lax.all_to_all(copies, ('layer', 'query'), 0, 0), axis=0)  16.3 us
    all_gather x1, waiting for transfers between devices, local(): eigen_rows = lax.all_gather(eigenvalues.T, 'doc', axis=0, tiled=True)  11 us
    all_to_all x1, starting transfers between devices, local(): rows = lax.all_to_all(copies, 'doc', 0, 0).reshape(queries, width)  4.77 us
    dot_general x1, matrix products, local(): part_out = jnp.dot(query_out, basis_out, preferred_element_type=jnp.float32)  3.54 us
  transfers between devices with their start and end apart: 2, of which 2 were waited for; matrix products, arithmetic and copies ran while one was open for 4% of the time, Pallas kernels for 0%

profile of v1, /device:TPU:3, one launch (start us, length us, event | category | flops | bytes accessed | tf_op | source)
XLA Modules:
  0.0 158.7 jit_solution(13439582940494309421)
XLA Ops:
  6.5 0.0 copy-start
  6.5 0.0 all-gather.2.cloned.1.call-start
  6.5 0.7 all-gather.2.cloned.1.call-update
  7.3 0.3 copy-done
  7.6 1.2 fusion.1
  8.8 3.5 %fusion.2 = f32[256,2752]{1,0:T(8,128)S(1)} fusion(bf16[256,688]{0,1:T(8,128)(2,1)} %param.9, bf16[688,2752]{1,0:T(8,128)(2,1)} %param.11), kind=kOutput, calls=%fused_computation.5 | convolution fusion | flops 969408512 | bytes 6957056 | tf_op jit(solution)/shard_map/dot_general | solution.py:151
  12.3 0.3 fusion
  12.7 37.4 %all_to_all.15 = f16[16,16,3776]{2,1,0:T(8,128)(2,1)S(1)} all-to-all(f16[16,16,3776]{2,1,0:T(8,128)(2,1)S(1)} %fusion), channel_id=1, replica_groups=mesh['layer'=4,'query'=4,'doc'=16] {'doc'}, dimensions={0} | all-to-all | bytes 3866624 | tf_op jit(solution)/shard_map/all_to_all | solution.py:155
  50.1 0.0 copy-start.3
  50.1 0.0 copy-start.2
  50.1 0.3 convert_reduce_fusion
  50.4 1.4 broadcast_in_dim.4
  51.8 4.8 %all-to-all-start.1 = ((bf16[16,16,3776]{2,1,0:T(8,128)(2,1)}), bf16[16,16,3776]{2,1,0:T(8,128)(2,1)S(1)}, u32[]{:S(2)}, u32[]{:S(2)}) async-start(bf16[16,16,3776]{2,1,0:T(8,128)(2,1)} %broadcast_in_dim.4), calls=%async_computation.1 | async-start | bytes 3932160 | tf_op jit(solution)/shard_map/all_to_all | solution.py:158
  56.6 0.0 copy-done.3
  56.6 0.1 copy.15.pairs_ref
  57.3 36.8 %all-to-all-done.1 = bf16[16,16,3776]{2,1,0:T(8,128)(2,1)S(1)} async-done(((bf16[16,16,3776]{2,1,0:T(8,128)(2,1)}), bf16[16,16,3776]{2,1,0:T(8,128)(2,1)S(1)}, u32[]{:S(2)}, u32[]{:S(2)}) %all-to-all-start.1) | async-done | bytes 1933344 | tf_op jit(solution)/shard_map/all_to_all | solution.py:158
  94.2 11.0 %all-gather.2.cloned.1.call-done.eig_ref = bf16[1024,2752]{1,0:T(8,128)(2,1)} async-done(((bf16[64,2752]{1,0:T(8,128)(2,1)}), bf16[1024,2752]{1,0:T(8,128)(2,1)}) %all-gather.2.cloned.1.call-update) | async-done | bytes 5636112 | tf_op jit(solution)/shard_map/all_gather | solution.py:146
  105.2 0.0 copy-done.2
  105.2 0.0 copy-start.1
  105.2 1.4 copy-done.1
  106.6 28.2 %shard_map.91 = f32[8,128]{1,0:T(8,128)S(1)} custom-call(s32[4,2]{1,0:T(4,128)S(1)} %copy.15.pairs_ref, s32[1]{0:T(128)S(6)} %copy.17.count_ref, bf16[256,3776]{1,0:T(8,128)(2,1)S(1)} %bitcast.9, bf16[256,3776]{1,0:T(8,128)(2,1)S(1)} %bitcast.10, bf16[1024,2752]{1,0:T(8,128)(2,1)} %all-gather.2.cloned.1.call-done.eig_ref, ...), custom_call_target="tpu_custom_call" | custom-call | flops 23085449216 | bytes 10485760 | tf_op jit(solution)/shard_map/pallas_call | solution.py:113
  134.8 16.3 %all_to_all.16 = f32[16,8,128]{2,1,0:T(8,128)S(1)} all-to-all(f32[16,8,128]{2,1,0:T(8,128)S(1)} %broadcast_in_dim.5), channel_id=1, replica_groups=mesh['layer'=4,'query'=4,'doc'=16] {'layer','query'}, dimensions={0} | all-to-all | bytes 131072 | tf_op jit(solution)/shard_map/all_to_all | solution.py:162
  151.2 0.7 reshape.15
  (3 shorter events, 0.0 us)
Async XLA Ops:
  6.5 1.0 copy-start
  6.5 98.7 %all-gather.2.cloned.1.call-start = ((), (), s32[]{:S(2)}) async-start(), calls=%async_computation.3 | async-start | bytes 6127616 | tf_op jit(solution)/shard_map/all_gather | solution.py:146
  50.1 6.5 %copy-start.3 = (s32[4,2]{0,1:T(2,128)S(1)}, s32[4,2]{0,1:T(2,128)}, u32[]{:S(2)}) copy-start(s32[4,2]{0,1:T(2,128)} %param.16) | copy-start | bytes 100
  50.1 55.1 %copy-start.2 = (bf16[4,64,1024]{2,1,0:T(8,128)(2,1)S(1)}, bf16[4,64,1024]{2,1,0:T(8,128)(2,1)}, u32[]{:S(2)}) copy-start(bf16[4,64,1024]{2,1,0:T(8,128)(2,1)} %in_ref.1) | copy-start | bytes 1572868
  51.8 42.4 %all-to-all-start.1 = ((bf16[16,16,3776]{2,1,0:T(8,128)(2,1)}), bf16[16,16,3776]{2,1,0:T(8,128)(2,1)S(1)}, u32[]{:S(2)}, u32[]{:S(2)}) async-start(bf16[16,16,3776]{2,1,0:T(8,128)(2,1)} %broadcast_in_dim.4), calls=%async_computation.1 | async-start | bytes 3932160 | tf_op jit(solution)/shard_map/all_to_all | solution.py:158
  105.2 1.4 copy-start.1
Sparse Core Ops, SparseCore 0:
  9.8 95.3 all-gather.1

commit v2 on v0

v2 whole, which is shorter than its diff:
```python
import jax
import jax.numpy as jnp
from jax import lax
from jax.experimental import pallas as pl
from jax.experimental.pallas import tpu as pltpu
from jax.sharding import PartitionSpec as P

FACTOR_RANK = 32
QUERY_BLOCK = 2
DOC_BLOCK = 2
TILE = 256
LANES = 128
SIDE = 4
SCALE = 4096.0

damping = 0.1

BLOCKS, GROUPS, MINE, WANTED, QUERIES, DOCS, LIVE, SWAP, ORDER = 0, 4, 8, 9, 10, 14, 18, 19, 20


def arrange_kernel(plan, near_ref, far_ref, rows_ref, columns, *, swap):
    near = near_ref[...].astype(jnp.float32).T
    far = far_ref[...].astype(jnp.float32).T
    half = near.shape[1]
    if swap:
        keep = plan[SWAP] == 0
        near, far = jnp.where(keep, near, far), jnp.where(keep, far, near)
    columns[:, :half] = near
    columns[:, half:] = far
    count = SIDE * SIDE
    size = columns.shape[0] // count
    for place in range(count):
        source = pl.multiple_of(plan[ORDER + place] * size, size)
        rows_ref[place * size:(place + 1) * size, :] = columns[pl.ds(source, size), :].astype(jnp.bfloat16)


def arrange(plan, near, far, near_map, far_map, model, swap):
    half = 2 * FACTOR_RANK * QUERY_BLOCK
    return pl.pallas_call(
        lambda *refs: arrange_kernel(*refs, swap=swap),
        out_shape=jax.ShapeDtypeStruct((model, 2 * half), jnp.bfloat16),
        grid_spec=pltpu.PrefetchScalarGridSpec(
            num_scalar_prefetch=1,
            grid=(1,),
            in_specs=[pl.BlockSpec((half, model), near_map), pl.BlockSpec((half, model), far_map)],
            out_specs=pl.BlockSpec((model, 2 * half), lambda i, plan: (0, 0)),
            scratch_shapes=[pltpu.VMEM((model, 2 * half), jnp.float32)],
        ),
        compiler_params=pltpu.CompilerParams(vmem_limit_bytes=32 * 2**20),
        cost_estimate=pl.CostEstimate(flops=0, bytes_accessed=4 * model * half * 2, transcendentals=0),
    )(plan, near, far)


def score_kernel(plan, *refs, spread, last):
    own_ref, refs = refs[0], refs[1:]
    if last:
        far_ref, earlier_ref, refs = refs[0], refs[1], refs[2:]
    query_ref, doc_ref, doc_rows_ref = refs[:3]
    weight_refs = refs[3:3 + len(spread)]
    result_ref, weights, scaled, total, sems = refs[3 + len(spread):8 + len(spread)]
    step = pl.program_id(0)
    padded = doc_rows_ref.shape[1]
    first = own_ref.shape[1] - padded
    band = weights.shape[1]
    bands = max(spread) + 1
    if last:
        rows, first, half = refs[-1], 0, own_ref.shape[0]
        begin_place = jnp.where(step < bands - 1, plan[MINE], 0)
        end_place = plan[WANTED]
    else:
        rows, begin_place, end_place = own_ref, 0, plan[MINE]

    def fetch(which, start):
        offset = 0
        for number, place in enumerate(spread):
            if place == which:
                size = weight_refs[number].shape[0]
                copy = pltpu.make_async_copy(
                    weight_refs[number], weights.at[which % 2, pl.ds(offset, size)], sems.at[number]
                )
                copy.start() if start else copy.wait()
                offset += size

    @pl.when(step == 0)
    def _():
        fetch(0, True)
        if last:
            total[...] = earlier_ref[...]
            rows[:half] = own_ref[:, own_ref.shape[1] - padded:]
            rows[half:] = far_ref[...]
        else:
            total[...] = jnp.zeros_like(total)

    for which in range(bands):
        @pl.when(step == which)
        def _():
            fetch(which, False)
            if which + 1 < bands:
                fetch(which + 1, True)

    slot = lax.rem(step, 2)
    query_side = query_ref[...]
    doc_side = doc_ref[...].astype(jnp.float32)
    lane = lax.broadcasted_iota(jnp.int32, query_side.shape, 1) // FACTOR_RANK
    empty = jnp.zeros_like(query_side)

    @pl.loop(begin_place, end_place)
    def _(place):
        block = plan[BLOCKS + place]
        left = jnp.concatenate(
            [
                jnp.where(lane == plan[GROUPS + place] + q, query_side, empty)
                for q in range(QUERY_BLOCK)
            ],
            axis=0,
        )
        for begin in range(0, padded, TILE):
            end = begin + TILE
            product = jnp.dot(
                left, rows[:, first + begin:first + end], preferred_element_type=jnp.float32
            )
            for q in range(QUERY_BLOCK):
                part = slice(q * band, (q + 1) * band)
                scaled[part, begin:end] = (product[part] * weights[slot, :, begin:end]).astype(jnp.bfloat16)
        mixed = lax.dot_general(
            scaled[...], doc_rows_ref[...], (((1,), (1,)), ((), ())), preferred_element_type=jnp.float32,
        )
        for q in range(QUERY_BLOCK):
            part = mixed[q * band:(q + 1) * band] * doc_side
            row = block * QUERY_BLOCK + q
            total[pl.ds(row, 1), :] += jnp.sum(part, axis=0, keepdims=True)

    @pl.when(step == bands - 1)
    def _():
        if not last:
            result_ref[...] = total[...]
            return
        sums = total[...]
        row = lax.broadcasted_iota(jnp.int32, sums.shape, 0)
        doc = lax.broadcasted_iota(jnp.int32, sums.shape, 1) // FACTOR_RANK
        query = jnp.full(sums.shape, -1, jnp.int32)
        block = jnp.full(sums.shape, -1, jnp.int32)
        for number in range(sums.shape[0] // QUERY_BLOCK):
            here = (row // QUERY_BLOCK == number) & (plan[LIVE] > number)
            query = jnp.where(here, plan[QUERIES + number] * QUERY_BLOCK + row % QUERY_BLOCK, query)
            block = jnp.where(here, plan[DOCS + number], block)
        picked = jnp.zeros_like(sums)
        for number in range(sums.shape[0]):
            picked = jnp.where(query == number, sums[number:number + 1], picked)
        column = lax.broadcasted_iota(jnp.int32, result_ref.shape, 1)
        result = jnp.zeros(result_ref.shape, jnp.float32)
        for d in range(DOC_BLOCK):
            value = jnp.sum(
                jnp.where(doc == block * DOC_BLOCK + d, picked, 0.0), axis=1, keepdims=True
            )
            result = jnp.where(column == d, value, result)
        result_ref[...] = result


def slot_scores(plan, own, query_side, doc_side, doc_rows, weights, spread, rest=()):
    model, queries = query_side.shape
    docs = doc_side.shape[1]
    last = bool(rest)
    padded = doc_rows.shape[1]
    bands = max(spread) + 1
    band = sum(rows.shape[0] for rows, place in zip(weights, spread) if place == 0)
    lanes = queries if last else queries // 2
    out_rows = queries // FACTOR_RANK
    whole = lambda array: pl.BlockSpec(array.shape, lambda j, plan: (0, 0))
    in_specs = [whole(array) for array in (own, *rest)] + [
        pl.BlockSpec((band, lanes), lambda j, plan: (j, 0)),
        pl.BlockSpec((band, docs), lambda j, plan: (j, 0)),
        whole(doc_rows),
    ] + [pl.BlockSpec(memory_space=pltpu.HBM)] * len(weights)
    shape = (out_rows, LANES if last else docs)
    scratch = [
        pltpu.VMEM((2, band, padded), jnp.float32),
        pltpu.VMEM((QUERY_BLOCK * band, padded), jnp.bfloat16),
        pltpu.VMEM((out_rows, docs), jnp.float32),
        pltpu.SemaphoreType.DMA((len(weights),)),
    ]
    if last:
        scratch.append(pltpu.VMEM((queries, padded), jnp.bfloat16))
    return pl.pallas_call(
        lambda *refs: score_kernel(*refs, spread=spread, last=last),
        out_shape=jax.ShapeDtypeStruct(shape, jnp.float32),
        grid_spec=pltpu.PrefetchScalarGridSpec(
            num_scalar_prefetch=1,
            grid=(bands,),
            in_specs=in_specs,
            out_specs=pl.BlockSpec(shape, lambda j, plan: (0, 0)),
            scratch_shapes=scratch,
        ),
        compiler_params=pltpu.CompilerParams(
            dimension_semantics=("arbitrary",), vmem_limit_bytes=40 * 2**20
        ),
        cost_estimate=pl.CostEstimate(
            flops=2 * 2 * 2 * QUERY_BLOCK * bands * band * queries * padded,
            bytes_accessed=4 * bands * band * padded + 4 * 2**20, transcendentals=0,
        ),
    )(plan, own, *rest, query_side, doc_side, doc_rows, *weights)


def make_plan(pair_list, pair_count, blocks, half, swap, order):
    slots = pair_list.shape[0]
    number = jnp.arange(blocks, dtype=jnp.int32)
    names = (number + half * (blocks // 2)) % blocks
    live = jnp.arange(slots, dtype=jnp.int32) < pair_count[0]
    chosen = pair_list[:, 0]
    wanted = jnp.any(live[:, None] & (chosen[:, None] == names[None]), axis=0)
    ones = wanted.astype(jnp.int32)
    place = jnp.sum(jnp.where(number[None] < number[:, None], ones[None], 0), axis=1)
    here = wanted[None] & (place[None] == number[:, None])
    listed = jnp.sum(jnp.where(here, names[None], 0), axis=1)
    groups = jnp.sum(jnp.where(here, number[None], 0), axis=1) * QUERY_BLOCK
    mine = jnp.sum(ones[:blocks // 2])[None]
    total = jnp.sum(ones)[None]
    return jnp.concatenate(
        [listed, groups, mine, total, chosen, pair_list[:, 1], pair_count, swap[None], order]
    ).astype(jnp.int32)


def local(
    query_out, query_in, basis_out, basis_in, eigenvalues, doc_out, doc_in, pair_list, pair_count
):
    layer, query, doc = (lax.axis_index(axis) for axis in ("layer", "query", "doc"))
    parts = lax.axis_size("doc")
    core = layer % 2
    odd = query % 2
    y, x = doc // SIDE, doc % SIDE
    model = doc_in.shape[2]

    def shift(array, by, first):
        pairs = []
        for source in range(lax.axis_size("layer") * parts):
            at, (row, column) = source // parts, divmod(source % parts, SIDE)
            if (at % 2 == 0) == first:
                column = (column + by) % SIDE
            else:
                row = (row + by) % SIDE
            pairs.append((source, at * parts + row * SIDE + column))
        return lax.ppermute(array, ("layer", "doc"), pairs)

    steps = jnp.array([0, -1, 1, 2], jnp.int32)
    near = (jnp.where(core == 0, x, y) + steps) % SIDE
    far = (jnp.where(core == 0, y, x) + steps) % SIDE
    order = jnp.where(
        core == 0, far[:, None] * SIDE + near[None], near[None] * SIDE + far[:, None]
    ).reshape(-1)
    blocks = query_out.shape[0] // (QUERY_BLOCK * FACTOR_RANK)
    plan = make_plan(pair_list, pair_count, blocks, odd, (core != odd).astype(jnp.int32), order)

    tail = -eigenvalues.shape[0] % TILE
    own_rows = eigenvalues.T
    left, right, across = (shift(own_rows, by, True) for by in (1, -1, 2))
    merge = lambda *rows: jnp.pad(
        jnp.concatenate(rows, axis=0), ((0, 0), (0, tail)), constant_values=1
    )
    top, bottom = merge(own_rows, left), merge(right, across)

    half = query_out.shape[0] // 2
    share = half // parts
    part_in = jnp.dot(
        lax.dynamic_slice_in_dim(query_in, core * half, half, 0), basis_in,
        preferred_element_type=jnp.float32,
    )
    part_out = jnp.dot(
        lax.dynamic_slice_in_dim(query_out, odd * half, half, 0), basis_out,
        preferred_element_type=jnp.float32,
    )
    partial = jnp.concatenate([part_in, jnp.pad(part_out, ((0, 0), (0, tail)))], axis=1)
    width = partial.shape[1]
    sent = (partial * SCALE).astype(jnp.float16).reshape(parts, share, width)
    received = lax.all_to_all(sent, "doc", 0, 0)
    summed = (jnp.sum(received.astype(jnp.float32), axis=0) * (1.0 / SCALE)).astype(jnp.bfloat16)

    doc_rows = jnp.pad(doc_out.reshape(-1, doc_out.shape[2]), ((0, 0), (0, tail)))
    in_rows = doc_in.reshape(-1, model)
    doc_side = arrange(
        plan, in_rows, in_rows, lambda i, plan: (0, 0), lambda i, plan: (1, 0), model, False
    )
    after = [shift(rows, 1, False) for rows in (top, bottom)]
    before = [shift(rows, -1, False) for rows in (top, bottom)]

    copies = jnp.broadcast_to(summed[None], (parts, share, width))
    own = lax.all_to_all(copies, "doc", 0, 0).reshape(half, width)
    swap = lambda axis: [(i, i ^ 1) for i in range(lax.axis_size(axis))]
    far_out = lax.ppermute(own[:, model:], "query", swap("query"))
    far_in = lax.ppermute(own[:, :model], "layer", swap("layer"))

    last = [shift(after[0], 1, False), shift(before[1], -1, False)]
    wait = summed[0, 0].astype(jnp.float32) * 0.0
    weights = [
        1.0 / (rows.astype(jnp.float32) + (damping + wait)) for rows in (top, bottom)
    ] + [1.0 / (rows.astype(jnp.float32) + damping) for rows in (*after, *before, *last)]
    spread = tuple(number // 2 for number in range(len(weights)))
    query_side = arrange(
        plan, own, far_in, lambda i, plan: (0, 0), lambda i, plan: (0, 0), model, True
    )
    sums = slot_scores(plan, own, query_side, doc_side, doc_rows, weights[:-2], spread[:-2])
    scores = slot_scores(
        plan, own, query_side, doc_side, doc_rows, weights, spread, (far_out, sums)
    )
    group = lax.axis_size("layer") * lax.axis_size("query")
    copies = jnp.broadcast_to(scores[None], (group,) + scores.shape)
    total = jnp.sum(lax.all_to_all(copies, ("layer", "query"), 0, 0), axis=0)
    return total[:, :DOC_BLOCK].reshape(pair_list.shape[0], QUERY_BLOCK * DOC_BLOCK)


def solution(mesh):
    in_specs = (
        P(None, "doc"),
        P(None, "doc"),
        P("doc", "layer"),
        P("doc", "query"),
        P("layer", ("query", "doc")),
        P("doc", None, "layer"),
        P("doc", None, "query"),
        P("doc", None),
        P("doc"),
    )
    out_specs = P("doc", None)
    return jax.shard_map(local, mesh=mesh, in_specs=in_specs, out_specs=out_specs, check_vma=False)
```

time: 579 us -> 128 us (0.22)
  the two profiles are of different devices: /device:TPU:5 before, /device:TPU:29 now
where the time goes in v2:
time: 128 us; the launch traced here: 129 us
  Pallas kernels  35.4 us (28%)
  starting transfers between devices  29.2 us (23%)
  other arithmetic  25.6 us (20%)
  blocking collectives  16.1 us (13%)
  local copies, waits for them, and re-layouts  8.76 us (7%)
  waiting for transfers between devices  8.72 us (7%)
  matrix products  3.19 us (2%)
  between operations  1.63 us (1%)
    pallas_call x2, Pallas kernels, slot_scores(): pl.pallas_call(lambda *refs: score_kernel(*refs, spread=spread, last=last...  33.8 us
    all_to_all x1, blocking collectives, local(): total = jnp.sum(lax.all_to_all(copies, ('layer', 'query'), 0, 0), axis=0)  16.1 us
    div x6, other arithmetic, local(): 1.0 / (rows.astype(jnp.float32) + damping)  12.6 us
    ppermute x9, waiting for transfers between devices, shift(): return lax.ppermute(array, ('layer', 'doc'), pairs)  8.71 us
    ppermute x9, starting transfers between devices, shift(): return lax.ppermute(array, ('layer', 'doc'), pairs)  8.03 us
    all_to_all x1, starting transfers between devices, local(): own = lax.all_to_all(copies, 'doc', 0, 0).reshape(half, width)  6.68 us
    all_to_all x1, starting transfers between devices, local(): received = lax.all_to_all(sent, 'doc', 0, 0)  6.51 us
    ppermute x1, starting transfers between devices, local(): far_in = lax.ppermute(own[:, :model], 'layer', swap('layer'))  6.1 us
  transfers between devices with their start and end apart: 13, of which 1 were waited for; matrix products, arithmetic and copies ran while one was open for 26% of the time, Pallas kernels for 11%

profile of v2, /device:TPU:29, one launch (start us, length us, event | category | flops | bytes accessed | tf_op | source)
XLA Modules:
  0.0 128.7 jit_solution(5059441115871507061)
XLA Ops:
  0.0 0.0 copy-start
  0.0 1.0 collective-permute-start.4
  1.0 0.0 collective-permute-start.3
  1.0 2.7 %collective-permute-start.2 = (bf16[64,2752]{1,0:T(8,128)(2,1)}, bf16[64,2752]{1,0:T(8,128)(2,1)}, u32[]{:S(2)}, u32[]{:S(2)}) collective-permute-start(bf16[64,2752]{1,0:T(8,128)(2,1)} %bitcast.30), channel_id=1, source_target_pairs={{0,1},{1,2},{2,3},{3,0},{4,5},{5,6},{6,7},{7,4},{8,9},{9,10},{10,1... | collective-permute-start | bytes 1056776 | tf_op jit(solution)/shard_map/ppermute | solution.py:242
  3.6 3.0 %fusion.7 = f32[128,2752]{1,0:T(8,128)S(1)} fusion(bf16[688,2752]{1,0:T(8,128)(2,1)} %param.12, bf16[256,688]{0,1:T(8,128)(2,1)} %param.10, s32[]{:T(128)S(6)} %select_n.87), kind=kOutput, calls=%fused_computation.20 | convolution fusion | flops 484704256 | bytes 5459972
  6.6 0.0 copy-start.10
  6.6 0.1 pad_bitcast_fusion
  6.7 0.8 copy-done.10
  7.5 0.2 convolution_bitcast_fusion
  7.7 1.2 fusion
  8.9 6.5 %all-to-all-start = ((f16[16,8,3840]{2,1,0:T(8,128)(2,1)}), f16[16,8,3840]{2,1,0:T(8,128)(2,1)}, u32[]{:S(2)}, u32[]{:S(2)}) async-start(f16[16,8,3840]{2,1,0:T(8,128)(2,1)} %fusion), calls=%async_computation | async-start | bytes 1966080 | tf_op jit(solution)/shard_map/all_to_all | solution.py:274
  16.2 0.1 and_reduce_fusion
  16.2 0.7 convert_reduce_fusion.1
  16.9 0.1 select_reduce_fusion.2
  17.0 0.1 add_select_fusion
  17.1 0.6 slice_reduce_fusion
  17.7 0.1 select_n.85
  17.8 0.1 select_reduce_fusion
  18.0 1.3 %concatenate.17.refs_0_ = s32[36]{0:T(128)S(1)} concatenate(s32[4]{0:T(128)S(1)} %get-tuple-element.6, s32[4]{0:T(128)S(1)} %broadcast_multiply_fusion, s32[1]{0:T(128)} %bitcast.2, s32[1]{0:T(128)} %bitcast.3, s32[4]{0:T(128)S(1)} %get-tuple-element.12, s32[4]{0:T(128)S(1)} %get-tuple-element.11, s32[1]{0:T(128)} %copy.15, s32[1]{0:T(128)} %bitcast.5, s32[16]{0:T(128)S(1)} %select_n.85), dimensions={0} | concatenate | bytes 288 | tf_op jit(solution)/shard_map/concatenate | solution.py:218
  19.3 0.8 shard_map.101.refs_3_.refs_5_
  20.1 1.5 %pad.16.refs_4_.refs_6_ = bf16[256,2816]{1,0:T(8,128)(2,1)S(1)} pad(bf16[256,2752]{1,0:T(8,128)(2,1)} %bitcast.33, bf16[]{:T(256)} %constant.96.clone.1), padding=0_0x0_64 | pad | bytes 2850818 | tf_op jit(solution)/shard_map/jit(_pad)/pad | solution.py:277
  21.6 0.0 copy-start.8
  21.6 0.0 collective-permute-done.4
  21.6 0.0 collective-permute-done.3
  21.6 2.1 %fusion.6 = bf16[128,2816]{1,0:T(8,128)(2,1)} fusion(bf16[64,2752]{1,0:T(8,128)(2,1)} %collective-permute-done.4, bf16[64,2752]{1,0:T(8,128)(2,1)} %collective-permute-done.3), kind=kLoop, calls=%fused_computation.19 | loop fusion | flops 2523136 | bytes 1425408 | tf_op jit(solution)/shard_map/concatenate | solution.py:257
  23.7 0.9 collective-permute-start.6
  24.6 0.6 collective-permute-start.8
  25.2 0.0 collective-permute-done.2
  25.2 1.9 %fusion.5 = bf16[128,2816]{1,0:T(8,128)(2,1)} fusion(bf16[64,2752]{1,0:T(8,128)(2,1)} %collective-permute-done.2, bf16[64,2752]{1,0:T(8,128)(2,1)S(1)} %bitcast.31), kind=kLoop, calls=%fused_computation.18 | loop fusion | flops 2523136 | bytes 1425408 | tf_op jit(solution)/shard_map/concatenate | solution.py:257
  27.1 0.9 collective-permute-start.5
  28.0 0.6 collective-permute-start.7
  28.6 0.0 all-to-all-done
  28.6 1.3 %convert_reduce_fusion = f32[8,3840]{1,0:T(8,128)S(1)} fusion(f16[16,8,3840]{2,1,0:T(8,128)(2,1)} %all-to-all-done), kind=kLoop, calls=%fused_computation.2 | loop fusion | flops 952320 | bytes 1105920 | tf_op jit(solution)/shard_map/reduce_sum | solution.py:275
  29.9 0.5 slice.30
  30.4 1.0 broadcast_in_dim.64
  31.5 6.7 %all-to-all-start.1 = ((bf16[16,8,3840]{2,1,0:T(8,128)(2,1)}), bf16[16,8,3840]{2,1,0:T(8,128)(2,1)S(1)}, u32[]{:S(2)}, u32[]{:S(2)}) async-start(bf16[16,8,3840]{2,1,0:T(8,128)(2,1)} %broadcast_in_dim.64), calls=%async_computation.1 | async-start | bytes 1966080 | tf_op jit(solution)/shard_map/all_to_all | solution.py:286
  38.8 2.4 %add_divide_fusion.6.refs_6_.refs_8_ = f32[128,2816]{1,0:T(8,128)} fusion(f32[]{:T(128)} %bitcast.12, bf16[64,2752]{1,0:T(8,128)(2,1)} %collective-permute-done.4, bf16[64,2752]{1,0:T(8,128)(2,1)} %collective-permute-done.3), kind=kLoop, calls=%fused_computation.15 | loop fusion | flops 3244032 | bytes 2146308 | tf_op jit(solution)/shard_map/div | solution.py:294
  41.2 2.3 %add_divide_fusion.7.refs_5_.refs_7_ = f32[128,2816]{1,0:T(8,128)} fusion(f32[]{:T(128)} %bitcast.12, bf16[64,2752]{1,0:T(8,128)(2,1)} %collective-permute-done.2, bf16[64,2752]{1,0:T(8,128)(2,1)S(1)} %bitcast.32), kind=kLoop, calls=%fused_computation.16 | loop fusion | flops 3244032 | bytes 2146308 | tf_op jit(solution)/shard_map/div | solution.py:294
  43.5 0.0 collective-permute-done.5
  43.5 1.0 collective-permute-start.9
  44.5 2.5 %add_divide_fusion.5.refs_7_.refs_9_ = f32[128,2816]{1,0:T(8,128)} fusion(bf16[128,2816]{1,0:T(8,128)(2,1)} %collective-permute-done.5), kind=kLoop, calls=%fused_computation.14 | loop fusion | flops 1081344 | bytes 2162688 | tf_op jit(solution)/shard_map/div | solution.py:295
  46.9 0.0 collective-permute-done.8
  46.9 0.5 collective-permute-start.10
  47.4 2.5 %add_divide_fusion.2.refs_10_.refs_12_ = f32[128,2816]{1,0:T(8,128)} fusion(bf16[128,2816]{1,0:T(8,128)(2,1)} %collective-permute-done.8), kind=kLoop, calls=%fused_computation.11 | loop fusion | flops 1081344 | bytes 2162688 | tf_op jit(solution)/shard_map/div | solution.py:295
  50.0 0.0 collective-permute-done.6
  50.0 2.4 %add_divide_fusion.4.refs_8_.refs_10_ = f32[128,2816]{1,0:T(8,128)} fusion(bf16[128,2816]{1,0:T(8,128)(2,1)} %collective-permute-done.6), kind=kLoop, calls=%fused_computation.13 | loop fusion | flops 1081344 | bytes 2162688 | tf_op jit(solution)/shard_map/div | solution.py:295
  52.4 0.0 collective-permute-done.7
  52.4 2.5 %add_divide_fusion.3.refs_9_.refs_11_ = f32[128,2816]{1,0:T(8,128)} fusion(bf16[128,2816]{1,0:T(8,128)(2,1)} %collective-permute-done.7), kind=kLoop, calls=%fused_computation.12 | loop fusion | flops 1081344 | bytes 2162688 | tf_op jit(solution)/shard_map/div | solution.py:295
  54.9 8.7 %collective-permute-done.10 = bf16[128,2816]{1,0:T(8,128)(2,1)S(1)} collective-permute-done((bf16[128,2816]{1,0:T(8,128)(2,1)}, bf16[128,2816]{1,0:T(8,128)(2,1)S(1)}, u32[]{:S(2)}, u32[]{:S(2)}) %collective-permute-start.10) | collective-permute-done | bytes 720928 | tf_op jit(solution)/shard_map/ppermute | solution.py:242
  63.6 1.4 %add_divide_fusion.refs_14_ = f32[128,2816]{1,0:T(8,128)} fusion(bf16[128,2816]{1,0:T(8,128)(2,1)S(1)} %collective-permute-done.10), kind=kLoop, calls=%fused_computation.9 | loop fusion | flops 1081344 | bytes 2162688 | tf_op jit(solution)/shard_map/div | solution.py:295
  64.9 0.0 all-to-all-done.1
  64.9 6.1 %collective-permute-start.1 = (bf16[128,1024]{1,0:T(8,128)(2,1)S(1)}, bf16[128,1024]{1,0:T(8,128)(2,1)S(1)}, u32[]{:S(2)}, u32[]{:S(2)}) collective-permute-start(bf16[128,1024]{1,0:T(8,128)(2,1)S(1)} %slice.29), channel_id=1, source_target_pairs={{0,64},{64,0},{128,192},{192,128},{1,65},{65,1},{129,193},{193,129... | collective-permute-start | bytes 786440 | tf_op jit(solution)/shard_map/ppermute | solution.py:289
  71.0 0.0 collective-permute-done.9
  71.0 1.4 %add_divide_fusion.1.refs_13_ = f32[128,2816]{1,0:T(8,128)S(1)} fusion(bf16[128,2816]{1,0:T(8,128)(2,1)} %collective-permute-done.9), kind=kLoop, calls=%fused_computation.10 | loop fusion | flops 1081344 | bytes 2162688 | tf_op jit(solution)/shard_map/div | solution.py:295
  72.5 1.9 %collective-permute-start = (bf16[128,2816]{1,0:T(8,128)(2,1)S(1)}, bf16[128,2816]{1,0:T(8,128)(2,1)S(1)}, u32[]{:S(2)}, u32[]{:S(2)}) collective-permute-start(bf16[128,2816]{1,0:T(8,128)(2,1)S(1)} %slice.28), channel_id=1, source_target_pairs={{0,16},{16,0},{32,48},{48,32},{1,17},{17,1},{33,49},{49,33},{2,18}... | collective-permute-start | bytes 2162696 | tf_op jit(solution)/shard_map/ppermute | solution.py:288
  74.4 0.0 collective-permute-done.1.refs_2_
  74.5 0.8 shard_map.100.refs_2_.refs_4_
  75.3 1.4 %copy-done.6 = f32[128,2816]{1,0:T(8,128)S(1)} copy-done((f32[128,2816]{1,0:T(8,128)S(1)}, f32[128,2816]{1,0:T(8,128)}, u32[]{:S(2)}) %copy-start.6) | copy-done | bytes 1441816
  76.7 1.4 %copy-done.7 = f32[128,2816]{1,0:T(8,128)S(1)} copy-done((f32[128,2816]{1,0:T(8,128)S(1)}, f32[128,2816]{1,0:T(8,128)}, u32[]{:S(2)}) %copy-start.7) | copy-done | bytes 1441816
  78.0 13.0 %shard_map.102.refs_3_ = f32[8,256]{1,0:T(8,128)S(1)} custom-call(s32[36]{0:T(128)S(1)} %concatenate.17.refs_0_, bf16[128,3840]{1,0:T(8,128)(2,1)S(1)} %bitcast.24, bf16[1024,256]{1,0:T(8,128)(2,1)S(1)} %shard_map.100.refs_2_.refs_4_, bf16[1024,256]{1,0:T(8,128)(2,1)S(1)} %shard_map.101.refs_3_.refs_5_, bf16[256,2816]{1,0:T(8,128)(2,1)S(1)} %pad.16.refs_4_.refs_6_, ...), custom_call_target="tpu_custom_call" | custom-call | flops 8858370048 | bytes 12845056 | tf_op jit(solution)/shard_map/pallas_call | solution.py:184
  91.1 0.0 collective-permute-done.refs_2_
  91.1 20.8 %shard_map.103 = f32[8,128]{1,0:T(8,128)S(1)} custom-call(s32[36]{0:T(128)S(1)} %concatenate.17.refs_0_, bf16[128,3840]{1,0:T(8,128)(2,1)S(1)} %bitcast.25, bf16[128,2816]{1,0:T(8,128)(2,1)S(1)} %collective-permute-done.refs_2_, f32[8,256]{1,0:T(8,128)S(1)} %shard_map.102.refs_3_, bf16[1024,256]{1,0:T(8,128)(2,1)S(1)} %shard_map.100.refs_2_.refs_4_, ...), custom_call_target="tpu_custom_call" | custom-call | flops 11811160064 | bytes 15728640 | tf_op jit(solution)/shard_map/pallas_call | solution.py:184
  111.9 16.1 %all_to_all.15 = f32[16,8,128]{2,1,0:T(8,128)S(1)} all-to-all(f32[16,8,128]{2,1,0:T(8,128)S(1)} %broadcast_in_dim.65), channel_id=1, replica_groups=mesh['layer'=4,'query'=4,'doc'=16] {'layer','query'}, dimensions={0} | all-to-all | bytes 131072 | tf_op jit(solution)/shard_map/all_to_all | solution.py:306
  128.0 0.7 reshape.67
  (30 shorter events, 0.2 us)
Async XLA Ops:
  0.0 6.7 %copy-start = (bf16[256,1024]{1,0:T(8,128)(2,1)S(1)}, bf16[256,1024]{1,0:T(8,128)(2,1)}, u32[]{:S(2)}) copy-start(bf16[256,1024]{1,0:T(8,128)(2,1)} %param.13) | copy-start | bytes 1572868
  0.0 21.6 %collective-permute-start.4 = (bf16[64,2752]{1,0:T(8,128)(2,1)}, bf16[64,2752]{1,0:T(8,128)(2,1)}, u32[]{:S(2)}, u32[]{:S(2)}) collective-permute-start(bf16[64,2752]{1,0:T(8,128)(2,1)} %bitcast.28), channel_id=1, source_target_pairs={{0,2},{1,3},{2,0},{3,1},{4,6},{5,7},{6,4},{7,5},{8,10},{9,11},{10,... | collective-permute-start | bytes 1056776 | tf_op jit(solution)/shard_map/ppermute | solution.py:242
  1.0 20.6 %collective-permute-start.3 = (bf16[64,2752]{1,0:T(8,128)(2,1)}, bf16[64,2752]{1,0:T(8,128)(2,1)}, u32[]{:S(2)}, u32[]{:S(2)}) collective-permute-start(bf16[64,2752]{1,0:T(8,128)(2,1)} %bitcast.29), channel_id=1, source_target_pairs={{0,3},{1,0},{2,1},{3,2},{4,7},{5,4},{6,5},{7,6},{8,11},{9,8},{10,9... | collective-permute-start | bytes 1056776 | tf_op jit(solution)/shard_map/ppermute | solution.py:242
  1.0 24.2 %collective-permute-start.2 = (bf16[64,2752]{1,0:T(8,128)(2,1)}, bf16[64,2752]{1,0:T(8,128)(2,1)}, u32[]{:S(2)}, u32[]{:S(2)}) collective-permute-start(bf16[64,2752]{1,0:T(8,128)(2,1)} %bitcast.30), channel_id=1, source_target_pairs={{0,1},{1,2},{2,3},{3,0},{4,5},{5,6},{6,7},{7,4},{8,9},{9,10},{10,1... | collective-permute-start | bytes 1056776 | tf_op jit(solution)/shard_map/ppermute | solution.py:242
  6.6 0.9 copy-start.10
  8.9 7.2 %copy-start.11 = (s32[4,2]{0,1:T(2,128)S(1)}, s32[4,2]{0,1:T(2,128)}, u32[]{:S(2)}) copy-start(s32[4,2]{0,1:T(2,128)} %param.17) | copy-start | bytes 100
  8.9 7.2 %copy-start.12 = (s32[4]{0:T(128)S(1)}, s32[4]{0:T(128)}, u32[]{:S(2)}) copy-start(s32[4]{0:T(128)} %constant.102.clone) | copy-start | bytes 52
  8.9 10.4 %copy-start.1 = (bf16[4,64,1024]{2,1,0:T(8,128)(2,1)S(1)}, bf16[4,64,1024]{2,1,0:T(8,128)(2,1)}, u32[]{:S(2)}) copy-start(bf16[4,64,1024]{2,1,0:T(8,128)(2,1)} %param.16) | copy-start | bytes 1572868
  8.9 19.6 %all-to-all-start = ((f16[16,8,3840]{2,1,0:T(8,128)(2,1)}), f16[16,8,3840]{2,1,0:T(8,128)(2,1)}, u32[]{:S(2)}, u32[]{:S(2)}) async-start(f16[16,8,3840]{2,1,0:T(8,128)(2,1)} %fusion), calls=%async_computation | async-start | bytes 1966080 | tf_op jit(solution)/shard_map/all_to_all | solution.py:274
  21.6 3.6 %copy-start.8 = (bf16[2752,64]{0,1:T(8,128)(2,1)S(1)}, bf16[2752,64]{0,1:T(8,128)(2,1)}, u32[]{:S(2)}) copy-start(bf16[2752,64]{0,1:T(8,128)(2,1)} %param.14) | copy-start | bytes 1056772
  23.7 26.3 %collective-permute-start.6 = (bf16[128,2816]{1,0:T(8,128)(2,1)}, bf16[128,2816]{1,0:T(8,128)(2,1)}, u32[]{:S(2)}, u32[]{:S(2)}) collective-permute-start(bf16[128,2816]{1,0:T(8,128)(2,1)} %fusion.6), channel_id=1, source_target_pairs={{0,4},{1,5},{2,6},{3,7},{4,8},{5,9},{6,10},{7,11},{8,12},{9,13},{1... | collective-permute-start | bytes 2162696 | tf_op jit(solution)/shard_map/ppermute | solution.py:242
  24.6 22.4 %collective-permute-start.8 = (bf16[128,2816]{1,0:T(8,128)(2,1)}, bf16[128,2816]{1,0:T(8,128)(2,1)}, u32[]{:S(2)}, u32[]{:S(2)}) collective-permute-start(bf16[128,2816]{1,0:T(8,128)(2,1)} %fusion.6), channel_id=1, source_target_pairs={{0,12},{1,13},{2,14},{3,15},{4,0},{5,1},{6,2},{7,3},{8,4},{9,5},{1... | collective-permute-start | bytes 2162696 | tf_op jit(solution)/shard_map/ppermute | solution.py:242
  27.1 16.4 %collective-permute-start.5 = (bf16[128,2816]{1,0:T(8,128)(2,1)}, bf16[128,2816]{1,0:T(8,128)(2,1)}, u32[]{:S(2)}, u32[]{:S(2)}) collective-permute-start(bf16[128,2816]{1,0:T(8,128)(2,1)} %fusion.5), channel_id=1, source_target_pairs={{0,4},{1,5},{2,6},{3,7},{4,8},{5,9},{6,10},{7,11},{8,12},{9,13},{1... | collective-permute-start | bytes 2162696 | tf_op jit(solution)/shard_map/ppermute | solution.py:242
  28.0 24.4 %collective-permute-start.7 = (bf16[128,2816]{1,0:T(8,128)(2,1)}, bf16[128,2816]{1,0:T(8,128)(2,1)}, u32[]{:S(2)}, u32[]{:S(2)}) collective-permute-start(bf16[128,2816]{1,0:T(8,128)(2,1)} %fusion.5), channel_id=1, source_target_pairs={{0,12},{1,13},{2,14},{3,15},{4,0},{5,1},{6,2},{7,3},{8,4},{9,5},{1... | collective-permute-start | bytes 2162696 | tf_op jit(solution)/shard_map/ppermute | solution.py:242
  31.5 33.5 %all-to-all-start.1 = ((bf16[16,8,3840]{2,1,0:T(8,128)(2,1)}), bf16[16,8,3840]{2,1,0:T(8,128)(2,1)S(1)}, u32[]{:S(2)}, u32[]{:S(2)}) async-start(bf16[16,8,3840]{2,1,0:T(8,128)(2,1)} %broadcast_in_dim.64), calls=%async_computation.1 | async-start | bytes 1966080 | tf_op jit(solution)/shard_map/all_to_all | solution.py:286
  38.1 3.1 %copy-start.9 = (bf16[2752,64]{0,1:T(8,128)(2,1)S(1)}, bf16[2752,64]{0,1:T(8,128)(2,1)}, u32[]{:S(2)}) copy-start(bf16[2752,64]{0,1:T(8,128)(2,1)} %param.14) | copy-start | bytes 1056772
  43.5 27.5 %collective-permute-start.9 = (bf16[128,2816]{1,0:T(8,128)(2,1)}, bf16[128,2816]{1,0:T(8,128)(2,1)}, u32[]{:S(2)}, u32[]{:S(2)}) collective-permute-start(bf16[128,2816]{1,0:T(8,128)(2,1)} %collective-permute-done.5), channel_id=1, source_target_pairs={{0,4},{1,5},{2,6},{3,7},{4,8},{5,9},{6,10},{7,11},{8,12},{9,13},{1... | collective-permute-start | bytes 2162696 | tf_op jit(solution)/shard_map/ppermute | solution.py:242
  46.9 16.6 %collective-permute-start.10 = (bf16[128,2816]{1,0:T(8,128)(2,1)}, bf16[128,2816]{1,0:T(8,128)(2,1)S(1)}, u32[]{:S(2)}, u32[]{:S(2)}) collective-permute-start(bf16[128,2816]{1,0:T(8,128)(2,1)} %collective-permute-done.8), channel_id=1, source_target_pairs={{0,12},{1,13},{2,14},{3,15},{4,0},{5,1},{6,2},{7,3},{8,4},{9,5},{1... | collective-permute-start | bytes 2162696 | tf_op jit(solution)/shard_map/ppermute | solution.py:242
  64.9 10.4 %copy-start.5 = (f32[128,2816]{1,0:T(8,128)S(1)}, f32[128,2816]{1,0:T(8,128)}, u32[]{:S(2)}) copy-start(f32[128,2816]{1,0:T(8,128)} %add_divide_fusion.2.refs_10_.refs_12_) | copy-start | bytes 4325380
  64.9 9.5 %collective-permute-start.1 = (bf16[128,1024]{1,0:T(8,128)(2,1)S(1)}, bf16[128,1024]{1,0:T(8,128)(2,1)S(1)}, u32[]{:S(2)}, u32[]{:S(2)}) collective-permute-start(bf16[128,1024]{1,0:T(8,128)(2,1)S(1)} %slice.29), channel_id=1, source_target_pairs={{0,64},{64,0},{128,192},{192,128},{1,65},{65,1},{129,193},{193,129... | collective-permute-start | bytes 786440 | tf_op jit(solution)/shard_map/ppermute | solution.py:289
  71.0 4.2 %copy-start.4 = (f32[128,2816]{1,0:T(8,128)S(1)}, f32[128,2816]{1,0:T(8,128)}, u32[]{:S(2)}) copy-start(f32[128,2816]{1,0:T(8,128)} %add_divide_fusion.5.refs_7_.refs_9_) | copy-start | bytes 4325380
  72.5 2.8 %copy-start.2 = (f32[128,2816]{1,0:T(8,128)S(1)}, f32[128,2816]{1,0:T(8,128)}, u32[]{:S(2)}) copy-start(f32[128,2816]{1,0:T(8,128)} %add_divide_fusion.6.refs_6_.refs_8_) | copy-start | bytes 4325380
  72.5 2.8 %copy-start.3 = (f32[128,2816]{1,0:T(8,128)S(1)}, f32[128,2816]{1,0:T(8,128)}, u32[]{:S(2)}) copy-start(f32[128,2816]{1,0:T(8,128)} %add_divide_fusion.7.refs_5_.refs_7_) | copy-start | bytes 4325380
  72.5 18.5 %collective-permute-start = (bf16[128,2816]{1,0:T(8,128)(2,1)S(1)}, bf16[128,2816]{1,0:T(8,128)(2,1)S(1)}, u32[]{:S(2)}, u32[]{:S(2)}) collective-permute-start(bf16[128,2816]{1,0:T(8,128)(2,1)S(1)} %slice.28), channel_id=1, source_target_pairs={{0,16},{16,0},{32,48},{48,32},{1,17},{17,1},{33,49},{49,33},{2,18}... | collective-permute-start | bytes 2162696 | tf_op jit(solution)/shard_map/ppermute | solution.py:288
  75.3 1.4 %copy-start.6 = (f32[128,2816]{1,0:T(8,128)S(1)}, f32[128,2816]{1,0:T(8,128)}, u32[]{:S(2)}) copy-start(f32[128,2816]{1,0:T(8,128)} %add_divide_fusion.4.refs_8_.refs_10_) | copy-start | bytes 4325380
  76.7 1.4 %copy-start.7 = (f32[128,2816]{1,0:T(8,128)S(1)}, f32[128,2816]{1,0:T(8,128)}, u32[]{:S(2)}) copy-start(f32[128,2816]{1,0:T(8,128)} %add_divide_fusion.3.refs_9_.refs_11_) | copy-start | bytes 4325380
